TPU v7x, 128 devices: a whole 4x4x4 slice. The times are simulated.
128 devices in a mesh: vel: 4 (over x_lo, core), gx: 16 (over z, y), gy: 2 (over x_hi).
Axes of the slice: x: 4 (x_hi: 2, x_lo: 2; x = x_hi * 2 + x_lo), y: 4, z: 4, core: 2. Of those that a mesh axis runs over, the one named last changes fastest.
Arguments:
- previous: bfloat16 [4096, 128, 256], P('vel', 'gx', 'gy'), may hold values from 0 to 4, as said below
- relax_time: float32 [128, 256], P('gx', 'gy'), may hold values from 0.05 to 20
- left_right_kind: int32 [2, 256], P(None, 'gy'), may hold values from 0 to 1
- bottom_top_kind: int32 [2, 128], P(None, 'gx'), may hold values from 0 to 1
- left_right_inflow: bfloat16 [4096, 2, 256], P('vel', None, 'gy'), may hold values from 0.049804688 to 1
- bottom_top_inflow: bfloat16 [4096, 2, 128], P('vel', None, 'gx'), may hold values from 0.049804688 to 1
Outputs:
- updated: bfloat16 [4096, 128, 256], P('vel', 'gx', 'gy')
Inputs may be any that keep to these rules, and one draw needn't show every extreme that they name: previous is positive in every entry. `left_right_kind`: 1 marks an inflow edge cell, 0 a diffuse wall. `bottom_top_kind`: 1 marks an inflow edge cell, 0 a diffuse wall.
All inputs are finite; a program needn't handle non-finite values.
Results may differ from a plain program's by a relative error of at most 0.0042.
Values may be sent and summed in bfloat16 or wider, within the bound.
A program may use at most 128 MiB of HBM per device.

v0:
```python
import functools
import math

import jax
import jax.numpy as jnp
import numpy as np
from jax import lax
from jax.experimental import pallas as pl
from jax.experimental.pallas import tpu as pltpu
from jax.sharding import PartitionSpec as P

NVX = 64
HALF = NVX // 2
NEWTON = 2
SWEEPS = 4
CHUNKS = 4
STEP = 12.0 / NVX
WEIGHT = STEP * STEP / (2.0 * math.pi)
DT_INV = (NVX - 1) * STEP / 100.0
PITCH = 9

NODES = (np.arange(NVX) - (NVX - 1) / 2.0) * STEP
ABS = [float((j + 0.5) * STEP) for j in range(HALF)]
WALL_1D = np.exp(-NODES * NODES / 2.0)
WALL_NORM = float(np.sum(np.maximum(NODES, 0.0) * WALL_1D) * np.sum(WALL_1D) * WEIGHT)
FLUX_SCALE = WEIGHT / WALL_NORM

F32 = jnp.float32
BF16 = jnp.bfloat16
MESH = pl.DeviceIdType.MESH


def dot_nt(a, b, **kw):
    return lax.dot_general(a, b, (((1,), (1,)), ((), ())), preferred_element_type=F32, **kw)


def dot_tn(a, b, **kw):
    return lax.dot_general(a, b, (((0,), (0,)), ((), ())), preferred_element_type=F32, **kw)


def loop(low, high, step):
    lax.fori_loop(low, high, lambda n, carry: (step(n), carry)[1], 0)


def iota(shape, dim):
    return lax.broadcasted_iota(jnp.int32, shape, dim)


def one_dim(lin, quad):
    top = None
    size = jnp.abs(lin)
    for x in ABS:
        e = (size + quad * x) * x
        top = e if top is None else jnp.maximum(top, e)
    for x in ABS:
        even = quad * (x * x) - top
        odd = lin * x
        yield x, jnp.exp(even + odd), jnp.exp(even - odd)
    yield None, top, None


def power_sums(lin, quad):
    sums = [None] * 5
    top = None
    for x, plus, minus in one_dim(lin, quad):
        if x is None:
            top = plus
            break
        s, d = plus + minus, plus - minus
        for n in range(5):
            term = (s if n % 2 == 0 else d) * (x**n)
            sums[n] = term if sums[n] is None else sums[n] + term
    return sums, top


def start_params(u):
    rho = u[0]
    inv = 1.0 / rho
    ux, uy = u[1] * inv, u[2] * inv
    sq = ux * ux + uy * uy
    t = u[3] * inv - sq / 2.0
    it = 1.0 / t
    return jnp.log(rho * it) - sq * 0.5 * it, ux * it, uy * it, -it


def solve_four(hessian, gradient):
    m = [list(r) for r in hessian]
    t = list(gradient)
    inv = [None] * 4
    for p in range(4):
        inv[p] = 1.0 / m[p][p]
        for low in range(p + 1, 4):
            f = m[low][p] * inv[p]
            for c in range(p + 1, 4):
                m[low][c] = m[low][c] - f * m[p][c]
            t[low] = t[low] - f * t[p]
    r = [None] * 4
    for p in (3, 2, 1, 0):
        a = t[p]
        for c in range(p + 1, 4):
            a = a - m[p][c] * r[c]
        r[p] = a * inv[p]
    return r


def newton_step(p, u):
    s, top_x = power_sums(p[1], p[3] * 0.5)
    q, top_y = power_sums(p[2], p[3] * 0.5)
    c = jnp.exp(p[0] + top_x + top_y) * WEIGHT
    s = [c * a for a in s]
    w = [
        s[0] * q[0],
        s[1] * q[0],
        s[0] * q[1],
        (s[2] * q[0] + s[0] * q[2]) * 0.5,
        s[2] * q[0],
        s[1] * q[1],
        (s[3] * q[0] + s[1] * q[2]) * 0.5,
        s[0] * q[2],
        (s[2] * q[1] + s[0] * q[3]) * 0.5,
        (s[4] * q[0] + 2.0 * s[2] * q[2] + s[0] * q[4]) * 0.25,
    ]
    layout = [[0, 1, 2, 3], [1, 4, 5, 6], [2, 5, 7, 8], [3, 6, 8, 9]]
    corr = solve_four([[w[layout[a][b]] for b in range(4)] for a in range(4)], [w[a] - u[a] for a in range(4)])
    return tuple(p[a] - corr[a] for a in range(4))


def kernel(
    nv, nx, ny, rows,
    prev_h, relax, lrk, btk, lri, bti,
    out_h,
    prev, gmain, src, afac, invd, sr, sl, rr, rl, moms, momr,
    strip, ssrc, sinv, xg, yg, xsr, xsl, xrr, xrl, xpr, xpl, ysend, yrecv,
    fys, fyr, fxs, fxr, inf, tmp, infs, yinf, mwy, wyt, vxl, kinds, ins, par,
    ld, st, mom_s, mom_r, r_s, r_r, l_s, l_r, xr_s, xr_r, xl_s, xl_r,
    y_s, y_r, fy_s, fy_r, fx_s, fx_r,
):
    v, gx, gy = lax.axis_index("vel"), lax.axis_index("gx"), lax.axis_index("gy")
    kyn = rows // NVX
    per = kyn // CHUNKS
    up = v >= nv // 2
    first, last = gx == 0, gx == nx - 1
    not_first, not_last = gx > 0, gx < nx - 1
    edge = jnp.logical_or(first, last)
    upwind = lax.rem(v // (nv // 2) + gy, 2) == 1
    downwind = lax.rem(v // (nv // 2) + gy, 2) == 0
    roll_by = jnp.where(up, 1, 127)

    barrier = pltpu.get_barrier_semaphore()

    def greet(*dev):
        pl.semaphore_signal(barrier, inc=1, device_id=dev, device_id_type=MESH)

    for k in range(1, nv):
        greet(lax.rem(v + k, nv), gx, gy)
    greet(v, gx, 1 - gy)
    pl.when(not_first)(lambda: greet(v, gx - 1, gy))
    pl.when(not_last)(lambda: greet(v, gx + 1, gy))

    part = rows * 8 // CHUNKS

    def load(c):
        at = pl.ds(pl.multiple_of(c * part, part), part)
        return pltpu.make_async_copy(prev_h.at[at], prev.at[at], ld.at[c])

    for c in range(CHUNKS):
        load(c).start()

    def remote(s, d, ss, rs, *dev):
        return pltpu.make_async_remote_copy(s, d, ss, rs, device_id=dev, device_id_type=MESH)

    hrow = rows // 2 // CHUNKS

    def halo(s, c, side):
        at = pl.ds(pl.multiple_of(c * hrow, hrow), hrow)
        if side == 0:
            return remote(sr.at[s, at], rr.at[s, at], r_s.at[s, c], r_r.at[s, c], v, gx + 1, gy)
        return remote(sl.at[s, at], rl.at[s, at], l_s.at[s, c], l_r.at[s, c], v, gx - 1, gy)

    def shalo(s, side):
        if side == 0:
            return remote(xsr.at[s], xrr.at[s], xr_s.at[s], xr_r.at[s], v, gx + 1, gy)
        return remote(xsl.at[s], xrl.at[s], xl_s.at[s], xl_r.at[s], v, gx - 1, gy)

    def yhalo(s):
        return remote(ysend.at[s], yrecv.at[s], y_s.at[s], y_r.at[s], v, gx, 1 - gy)

    def moment(k):
        return remote(moms, momr.at[k - 1], mom_s.at[k - 1], mom_r.at[k - 1], lax.rem(v + k, nv), gx, gy)

    def fluxx(s, k):
        return remote(fxs.at[s], fxr.at[s, k - 1], fx_s.at[s, k - 1], fx_r.at[s, k - 1], lax.rem(v + k, nv), gx, gy)

    half = nv // 2

    def fluxy(s, k):
        mine = lax.rem(v, half)
        return remote(fys.at[s], fyr.at[s, mine], fy_s.at[s, k], fy_r.at[s, mine], (1 - v // half) * half + k, gx, gy)

    def fluxy_in(s, k):
        return remote(fys.at[s], fyr.at[s, k], fy_s.at[s, k], fy_r.at[s, k], (1 - v // half) * half + k, gx, gy)

    lane = iota((8, 128), 1)
    sub = iota((8, 128), 0)
    cell = lax.rem(lane, 8)
    in_tile = lane // 8
    irel = 1.0 / relax[...]

    def inv_of(m):
        at = pl.ds(pl.multiple_of(m * 8, 8), 8)
        invd[at, :] = 1.0 / (DT_INV + irel + (m + 1).astype(F32) * STEP)

    loop(0, NVX - 1, inv_of)
    for t in range(4):
        vxl[t * 8 : t * 8 + 8, :] = ((t * 16 + in_tile).astype(F32) - (NVX - 1) / 2.0) * STEP
    for b in range(kyn * 4 // 8):
        t = b * 8 + sub
        ky = (v * kyn + t // 4).astype(F32)
        yy = (ky - (NVX - 1) / 2.0) * STEP
        xx = ((lax.rem(t, 4) * 16 + in_tile).astype(F32) - (NVX - 1) / 2.0) * STEP
        at = slice(b * 8, b * 8 + 8)
        mwy[at, :] = jnp.exp((xx * xx + yy * yy) * -0.5)
        wyt[at, :] = jnp.abs(yy) * FLUX_SCALE
    posn = jnp.where(up, lane, 127 - lane)
    want = sub + jnp.where(sub >= 4, 120, 0)
    sel = (posn == want).astype(F32)
    sel16 = sel.astype(BF16)
    sel_up = jnp.where(sub < 4, sel, 0.0)
    in_strip = posn < 4
    rep8 = (cell == sub).astype(F32)

    pl.semaphore_wait(barrier, nv + not_first.astype(jnp.int32) + not_last.astype(jnp.int32))

    def gat(ky, off, stride=1):
        return pl.ds(ky * (NVX * PITCH) + off, 8, stride=stride)

    def pack_halo(ky, s):
        for q in range(0, HALF // 8, 2):
            right = [gmain[gat(ky, PITCH * (HALF + 8 * (q + d)) + 8, PITCH), :] for d in range(2)]
            left = [gmain[gat(ky, PITCH * 8 * (q + d), PITCH), :] for d in range(2)]
            at = pl.ds(pl.multiple_of(ky * HALF + q * 8, 16), 16)
            sr[s, at, :] = jnp.concatenate(right, axis=0).astype(BF16)
            sl[s, at, :] = jnp.concatenate(left, axis=0).astype(BF16)

    def send_chunk(s, c):
        pl.when(not_last)(lambda: halo(s, c, 0).start())
        pl.when(not_first)(lambda: halo(s, c, 1).start())

    def take_row(ky, u):
        base = pl.multiple_of(ky * (NVX * 8), NVX * 8)
        s0 = s1 = s2 = jnp.zeros((8, 128), F32)
        for i in range(0, HALF, 2):
            pos = prev[pl.ds(base + (HALF + i) * 8, 16), :].astype(F32)
            neg = prev[pl.ds(base + (HALF - 2 - i) * 8, 16), :].astype(F32)
            for d in range(2):
                a, b = pos[8 * d : 8 * d + 8], neg[8 - 8 * d : 16 - 8 * d]
                gmain[gat(ky, PITCH * (HALF + i + d) + 1), :] = a
                gmain[gat(ky, PITCH * (HALF - 1 - i - d)), :] = b
                x = ABS[i + d]
                both = a + b
                s0 = s0 + both
                s1 = s1 + (a - b) * x
                s2 = s2 + both * (x * x)
        yy = ((v * kyn + ky).astype(F32) - (NVX - 1) / 2.0) * STEP
        pack_halo(ky, 0)
        return (u[0] + s0, u[1] + s1, u[2] + s0 * yy, u[3] + (s2 + s0 * (yy * yy)) * 0.5)

    def take_chunk(c, u):
        load(c).wait()
        u = lax.fori_loop(c * per, c * per + per, take_row, u)
        send_chunk(0, c)
        return u

    zero = jnp.zeros((8, 128), F32)
    u = lax.fori_loop(0, CHUNKS, take_chunk, (zero, zero, zero, zero))
    for a in range(4):
        moms[a * 8 : a * 8 + 8, :] = u[a] * WEIGHT
    for k in range(1, nv):
        moment(k).start()

    def take_strip(ky):
        block = prev[pl.ds(pl.multiple_of(ky * 512, 512), 512), :]
        got = dot_nt(sel16, block)
        for t in range(4):
            strip[pl.ds(pl.multiple_of(ky * 32 + t * 8, 8), 8), :] = got[:, t * 128 : t * 128 + 128]

    loop(0, kyn, take_strip)

    def tile(ky, t):
        return pl.ds(pl.multiple_of(ky * 32 + t * 8, 8), 8)

    groups = kyn // 4

    def send_strips(s):
        def pack(g):
            right = left = jnp.zeros((8, 128), F32)
            for r in range(4):
                for h in range(2):
                    k = r * 2 + h
                    c = strip[tile(g * 4 + r, 2 + h), :]
                    right = jnp.where(cell == k, c if k == 7 else pltpu.roll(c, (k - 7) % 128, 1), right)
                    c = strip[tile(g * 4 + r, h), :]
                    left = jnp.where(cell == k, c if k == 0 else pltpu.roll(c, k, 1), left)
            at = pl.ds(pl.multiple_of(g * 8, 8), 8)
            xpr[at, :] = right
            xpl[at, :] = left

        loop(0, groups, pack)
        xsr[s] = xpr[...].astype(BF16)
        xsl[s] = xpl[...].astype(BF16)
        pl.when(not_last)(lambda: shalo(s, 0).start())
        pl.when(not_first)(lambda: shalo(s, 1).start())

        acc = jnp.zeros((8, 128), F32)
        for b in range(0, kyn * 4 // 8, 2):
            two = []
            for d in range(2):
                row = strip[pl.ds((b + d) * 64 + 7, 8, stride=8), :]
                acc = acc + row * wyt[(b + d) * 8 : (b + d) * 8 + 8, :]
                two.append(row)
            ysend[s, b * 8 : b * 8 + 16, :] = jnp.concatenate(two, axis=0).astype(BF16)
        fys[s] = acc

        @pl.when(upwind)
        def _():
            yhalo(s).start()

        @pl.when(downwind)
        def _():
            for k in range(half):
                fluxy(s, k).start()

    def send_edges(s):
        def partial(rows_ref, tile_off, spot):
            def add(ky, carry):
                main, thin = carry
                block = rows_ref[s, pl.ds(pl.multiple_of(ky * HALF, HALF), HALF), :].astype(F32)
                for q in range(HALF // 8):
                    j = (q * 8 + sub).astype(F32)
                    x = (j + 0.5) * STEP if tile_off else (HALF - 0.5 - j) * STEP
                    main = main + block[q * 8 : q * 8 + 8] * x
                for h in range(2):
                    c = strip[tile(ky, tile_off + h), :]
                    x = jnp.abs(vxl[(tile_off + h) * 8 : (tile_off + h) * 8 + 8, :])
                    thin = thin + c * jnp.where(cell == spot, x, 0.0)
                return main, thin

            main, thin = lax.fori_loop(0, kyn, add, (zero, zero))
            thin = jnp.broadcast_to(jnp.sum(thin, axis=1, keepdims=True), (8, 128)) * sel_up
            fxs[s] = (jnp.where(in_strip, 0.0, main) + thin) * FLUX_SCALE
            for k in range(1, nv):
                fluxx(s, k).start()

        pl.when(first)(lambda: partial(sl, 0, 0))
        pl.when(last)(lambda: partial(sr, 2, 7))

    send_strips(0)
    send_edges(0)

    @pl.when(edge)
    def _():
        side = jnp.where(first, 0, 1)
        off = jnp.where(first, HALF, 0)

        def take(ky):
            at = pl.ds(pl.multiple_of((ky * NVX + off) * 2, 2 * HALF), 2 * HALF)
            tmp[...] = lri[at, :].astype(F32)
            for q in range(HALF // 8):
                at = pl.ds(pl.multiple_of(ky * HALF + q * 8, 8), 8)
                inf[at, :] = tmp[pl.ds(q * 16 + side, 8, stride=2), :]

        loop(0, kyn, take)
        kind = jnp.where(first, lrk[0:1, :], lrk[1:2, :]).astype(F32)
        kinds[0:8, :] = jnp.broadcast_to(kind, (8, 128))
        kinds[8:16, :] = dot_nt(sel, jnp.broadcast_to(kind, (128, 128)))

        def spread(b):
            got = dot_nt(sel, inf[pl.ds(pl.multiple_of(b * 128, 128), 128), :])
            for w in range(8):
                rep = (iota((128, 128), 0) == w * 16 + iota((128, 128), 1) // 8).astype(F32)
                infs[pl.ds(pl.multiple_of(b * 64 + w * 8, 8), 8), :] = jnp.dot(got, rep, preferred_element_type=F32)

        loop(0, kyn * HALF // 128, spread)

    @pl.when(upwind)
    def _():
        side = jnp.where(up, 0, 1)
        row = iota((512, 128), 0)
        keep = jnp.logical_and(lax.rem(row, 2) == side, lax.rem(row // 2, 16) == iota((512, 128), 1) // 8)
        gather = (iota((16, 512), 1) // 32 == iota((16, 512), 0)).astype(F32)

        def take(b):
            block = bti[pl.ds(pl.multiple_of(b * 512, 512), 512), :].astype(F32)
            wide = jnp.dot(block, rep8, preferred_element_type=F32)
            wide = jnp.where(keep, wide, 0.0)
            yinf[pl.ds(pl.multiple_of(b * 16, 16), 16), :] = jnp.dot(gather, wide, preferred_element_type=F32)

        loop(0, rows * 2 // 512, take)
        kind = jnp.where(up, btk[0:1, :], btk[1:2, :]).astype(F32)
        kinds[16:24, :] = jnp.dot(jnp.broadcast_to(kind, (8, 8)), rep8, preferred_element_type=F32)

    for k in range(1, nv):
        moment(k).wait_recv()
    u = [moms[a * 8 : a * 8 + 8, :] for a in range(4)]
    for k in range(nv - 1):
        u = [u[a] + momr[k, a * 8 : a * 8 + 8, :] for a in range(4)]
    p = start_params(u)
    p = lax.fori_loop(0, NEWTON, lambda n, q: newton_step(q, u), p)

    pq = p[3] * 0.5
    top_x = None
    for j, (x, plus, minus) in enumerate(one_dim(p[1], pq)):
        if x is None:
            top_x = plus
        else:
            afac[(HALF + j) * 8 : (HALF + j) * 8 + 8, :] = plus
            afac[(HALF - 1 - j) * 8 : (HALF - j) * 8, :] = minus
    height = p[0] + top_x

    thin = [
        dot_nt(sel, jnp.broadcast_to(a[None], (16, 8, 128)).reshape(128, 128), precision=lax.Precision.HIGHEST)
        for a in (*p, irel)
    ]

    def speed_y(ky):
        return ((v * kyn + ky).astype(F32) - (NVX - 1) / 2.0) * STEP

    def edge_flux(s):
        total = fxs[s]
        for k in range(nv - 1):
            total = total + fxr[s, k]
        return jnp.broadcast_to(jnp.sum(total, axis=0, keepdims=True), (8, 128))

    def sweep_strips(s):
        @pl.when(not_first)
        def _():
            shalo(s, 0).wait_recv()
            xpr[...] = xrr[s].astype(F32)

            def put(g):
                c = xpr[pl.ds(pl.multiple_of(g * 8, 8), 8), :]
                for k in range(8):
                    xg[tile(g * 4 + k // 2, 2 + k % 2), :] = c if k == 0 else pltpu.roll(c, 128 - k, 1)

            loop(0, groups, put)

        @pl.when(not_last)
        def _():
            shalo(s, 1).wait_recv()
            xpl[...] = xrl[s].astype(F32)

            def put(g):
                c = xpl[pl.ds(pl.multiple_of(g * 8, 8), 8), :]
                for k in range(8):
                    xg[tile(g * 4 + k // 2, k % 2), :] = c if k == 7 else pltpu.roll(c, 7 - k, 1)

            loop(0, groups, put)

        @pl.when(edge)
        def _():
            for k in range(1, nv):
                fluxx(s, k).wait_recv()
            kind = kinds[8:16, :]
            flux = jnp.broadcast_to(jnp.sum(edge_flux(s) * sel, axis=1, keepdims=True), (8, 128)) * (1.0 - kind)

            def fill(ky, t0):
                for h in range(2):
                    wall = mwy[pl.ds(ky * 4 + t0 + h, 1), :]
                    inflow = infs[pl.ds(pl.multiple_of(ky * 16 + h * 8, 8), 8), :]
                    xg[tile(ky, t0 + h), :] = kind * inflow + flux * wall

            pl.when(first)(lambda: loop(0, kyn, lambda ky: fill(ky, 2)))
            pl.when(last)(lambda: loop(0, kyn, lambda ky: fill(ky, 0)))

        @pl.when(downwind)
        def _():
            yhalo(s).wait_recv()
            yg[...] = yrecv[s].astype(F32)

        @pl.when(upwind)
        def _():
            for k in range(half):
                fluxy_in(s, k).wait_recv()
            total = fyr[s, 0]
            for k in range(1, half):
                total = total + fyr[s, k]
            flux = jnp.broadcast_to(jnp.sum(total, axis=0, keepdims=True), (8, 128))
            for k in (8, 16, 32, 64):
                flux = flux + pltpu.roll(flux, k, 1)
            kind = kinds[16:24, :]
            flux = flux * (1.0 - kind)
            for b in range(kyn * 4 // 8):
                at = slice(b * 8, b * 8 + 8)
                yg[at, :] = kind * yinf[at, :] + flux * mwy[at, :]

        def step(ky):
            yy = speed_y(ky)
            ay = jnp.abs(yy)
            for t in range(4):
                c = strip[tile(ky, t), :]
                xx = vxl[t * 8 : t * 8 + 8, :]
                ax = jnp.abs(xx)
                if s == 0:
                    power = thin[0] + xx * thin[1] + yy * thin[2] + (xx * xx + yy * yy) * 0.5 * thin[3]
                    source = c * DT_INV + jnp.exp(power) * thin[4]
                    inv = 1.0 / (DT_INV + thin[4] + ax + ay)
                    ssrc[tile(ky, t), :] = source
                    sinv[tile(ky, t), :] = inv
                else:
                    source = ssrc[tile(ky, t), :]
                    inv = sinv[tile(ky, t), :]
                from_y = jnp.where(sub == 0, yg[pl.ds(ky * 4 + t, 1), :], pltpu.roll(c, 1, 0))
                if t >= 2:
                    from_x = jnp.where(cell == 0, xg[tile(ky, t), :], pltpu.roll(c, 1, 1))
                else:
                    from_x = jnp.where(cell == 7, xg[tile(ky, t), :], pltpu.roll(c, 127, 1))
                strip[tile(ky, t), :] = (source + ax * from_x + ay * from_y) * inv

        loop(0, kyn, step)

    def fill_main(s, c):
        @pl.when(not_first)
        def _():
            halo(s, c, 0).wait_recv()

            def put(ky):
                block = rr[s, pl.ds(pl.multiple_of(ky * HALF, HALF), HALF), :].astype(F32)
                for q in range(HALF // 8):
                    gmain[gat(ky, PITCH * (HALF + 8 * q), PITCH), :] = block[q * 8 : q * 8 + 8]

            loop(c * per, c * per + per, put)

        @pl.when(not_last)
        def _():
            halo(s, c, 1).wait_recv()

            def put(ky):
                block = rl[s, pl.ds(pl.multiple_of(ky * HALF, HALF), HALF), :].astype(F32)
                for q in range(HALF // 8):
                    gmain[gat(ky, PITCH * 8 * q + 8, PITCH), :] = block[q * 8 : q * 8 + 8]

            loop(c * per, c * per + per, put)

        @pl.when(edge)
        def _():
            kind = kinds[0:8, :]
            flux = edge_flux(s) * (1.0 - kind)

            def rows_of(ky, q, positive):
                j = (q * 8 + sub).astype(F32)
                x = (j + 0.5) * STEP if positive else (HALF - 0.5 - j) * STEP
                yy = speed_y(ky)
                wall = jnp.exp((x * x + yy * yy) * -0.5)
                return kind * inf[pl.ds(pl.multiple_of(ky * HALF + q * 8, 8), 8), :] + flux * wall

            def put_low(ky):
                for q in range(HALF // 8):
                    gmain[gat(ky, PITCH * (HALF + 8 * q), PITCH), :] = rows_of(ky, q, True)

            def put_high(ky):
                for q in range(HALF // 8):
                    gmain[gat(ky, PITCH * 8 * q + 8, PITCH), :] = rows_of(ky, q, False)

            pl.when(first)(lambda: loop(c * per, c * per + per, put_low))
            pl.when(last)(lambda: loop(c * per, c * per + per, put_high))

    def main_row(ky, s, b_of):
        yy = speed_y(ky)
        ay = jnp.abs(yy)
        kyg = v * kyn + ky
        jj = jnp.where(kyg >= HALF, kyg - HALF, HALF - 1 - kyg)
        base = pl.multiple_of(ky * (NVX * 8), NVX * 8)
        if s == 0:
            bfac = b_of(yy)
        for i in range(0, HALF, 2):
            inv = [invd[pl.ds(pl.multiple_of((jj + i + d) * 8, 8), 8), :] for d in range(2)]
            for positive in (True, False):
                done = []
                for d in range(2):
                    kx = HALF + i + d if positive else HALF - 1 - i - d
                    own_off = PITCH * kx + (1 if positive else 0)
                    own = gmain[gat(ky, own_off), :]
                    moved = gmain[gat(ky, PITCH * kx + (0 if positive else 1)), :]
                    turned = pltpu.roll(own, roll_by, 1)
                    at = pl.ds(base + kx * 8, 8)
                    if s == 0:
                        source = own * DT_INV + afac[kx * 8 : kx * 8 + 8, :] * bfac
                        src[at, :] = source
                    else:
                        source = src[at, :]
                    new = (source + moved * ABS[i + d] + turned * ay) * inv[d]
                    if s < SWEEPS - 1:
                        gmain[gat(ky, own_off), :] = new
                    else:
                        done.append(jnp.where(in_strip, ins[at, :], new))
                if s == SWEEPS - 1:
                    kx = HALF + i if positive else HALF - 2 - i
                    if not positive:
                        done = done[::-1]
                    prev[pl.ds(base + kx * 8, 16), :] = jnp.concatenate(done, axis=0).astype(BF16)

    def store(c):
        at = pl.ds(pl.multiple_of(c * part, part), part)
        return pltpu.make_async_copy(prev.at[at], out_h.at[at], st.at[c])

    size_y = jnp.abs(p[2])
    top_y = None
    for y in ABS:
        e = (size_y + pq * y) * y
        top_y = e if top_y is None else jnp.maximum(top_y, e)
    amp = jnp.exp(height + top_y) * irel

    def b_of(yy):
        return amp * jnp.exp((p[2] + pq * yy) * yy - top_y)

    for s in range(SWEEPS):
        sweep_strips(s)
        if s < SWEEPS - 1:
            send_strips(s + 1)
        else:

            def put(ky):
                for t in range(4):
                    at = pl.ds(pl.multiple_of(ky * 512 + t * 128, 128), 128)
                    ins[at, :] = dot_tn(strip[tile(ky, t), :], sel_up)

            loop(0, kyn, put)

        def chunk(c):
            fill_main(s, c)

            def one(ky):
                main_row(ky, s, b_of)
                if s < SWEEPS - 1:
                    pack_halo(ky, s + 1)

            loop(c * per, c * per + per, one)
            if s < SWEEPS - 1:
                send_chunk(s + 1, c)
            else:
                store(c).start()

        loop(0, CHUNKS, chunk)
        if s < SWEEPS - 1:
            send_edges(s + 1)

    for k in range(1, nv):
        moment(k).wait_send()

    def drain(s):
        def both(c):
            pl.when(not_last)(lambda: halo(s, c, 0).wait_send())
            pl.when(not_first)(lambda: halo(s, c, 1).wait_send())

        loop(0, CHUNKS, both)
        pl.when(not_last)(lambda: shalo(s, 0).wait_send())
        pl.when(not_first)(lambda: shalo(s, 1).wait_send())
        pl.when(upwind)(lambda: yhalo(s).wait_send())

        @pl.when(downwind)
        def _():
            for k in range(half):
                fluxy(s, k).wait_send()

        @pl.when(edge)
        def _():
            for k in range(1, nv):
                fluxx(s, k).wait_send()


    loop(0, SWEEPS, drain)
    for c in range(CHUNKS):
        store(c).wait()


def body(previous, relax_time, left_right_kind, bottom_top_kind, left_right_inflow, bottom_top_inflow, *, sizes):
    nv, nx, ny = sizes
    rows, cx, cy = previous.shape
    kyn = rows // NVX
    thin = rows * 8 // 128 * 8
    dma = pltpu.SemaphoreType.DMA
    vm = pltpu.VMEM
    hr = rows // 2
    ur = kyn * 4
    xr = kyn * 2
    scratch = [
        vm((rows * 8, 128), BF16), vm((rows * PITCH, 128), F32), vm((rows * 8, 128), F32),
        vm((NVX * 8, 128), F32), vm((NVX * 8, 128), F32),
        vm((SWEEPS, hr, 128), BF16), vm((SWEEPS, hr, 128), BF16),
        vm((SWEEPS, hr, 128), BF16), vm((SWEEPS, hr, 128), BF16),
        vm((32, 128), F32), vm((nv - 1, 32, 128), F32),
        vm((thin, 128), F32), vm((thin, 128), F32), vm((thin, 128), F32), vm((thin, 128), F32),
        vm((ur, 128), F32),
        vm((SWEEPS, xr, 128), BF16), vm((SWEEPS, xr, 128), BF16),
        vm((SWEEPS, xr, 128), BF16), vm((SWEEPS, xr, 128), BF16),
        vm((xr, 128), F32), vm((xr, 128), F32),
        vm((SWEEPS, ur, 128), BF16), vm((SWEEPS, ur, 128), BF16),
        vm((SWEEPS, 8, 128), F32), vm((SWEEPS, nv // 2, 8, 128), F32),
        vm((SWEEPS, 8, 128), F32), vm((SWEEPS, nv - 1, 8, 128), F32),
        vm((hr, 128), F32), vm((NVX, 128), F32), vm((thin // 2, 128), F32),
        vm((ur, 128), F32), vm((ur, 128), F32), vm((ur, 128), F32),
        vm((32, 128), F32), vm((24, 128), F32), vm((rows * 8, 128), F32), vm((8, 128), F32),
        dma((CHUNKS,)), dma((CHUNKS,)), dma((nv - 1,)), dma((nv - 1,)),
        dma((SWEEPS, CHUNKS)), dma((SWEEPS, CHUNKS)), dma((SWEEPS, CHUNKS)), dma((SWEEPS, CHUNKS)),
        dma((SWEEPS,)), dma((SWEEPS,)), dma((SWEEPS,)), dma((SWEEPS,)),
        dma((SWEEPS,)), dma((SWEEPS,)), dma((SWEEPS, nv // 2)), dma((SWEEPS, nv // 2)),
        dma((SWEEPS, nv - 1)), dma((SWEEPS, nv - 1)),
    ]
    whole = pl.BlockSpec(memory_space=pltpu.VMEM)
    far = pl.BlockSpec(memory_space=pl.ANY)
    out = pl.pallas_call(
        functools.partial(kernel, nv, nx, ny, rows),
        out_shape=jax.ShapeDtypeStruct((rows * 8, 128), BF16),
        in_specs=[far, whole, whole, whole, whole, whole],
        out_specs=far,
        scratch_shapes=scratch,
        compiler_params=pltpu.CompilerParams(
            collective_id=0, has_side_effects=True, vmem_limit_bytes=48 * 1024 * 1024
        ),
        name="bgk_step",
    )(
        previous.reshape(rows * 8, 128),
        relax_time,
        left_right_kind,
        bottom_top_kind,
        left_right_inflow.reshape(rows * 2, 128),
        bottom_top_inflow.reshape(rows * 2, 8),
    )
    return out.reshape(rows, cx, cy)


def solution(mesh):
    sizes = (mesh.shape["vel"], mesh.shape["gx"], mesh.shape["gy"])
    return jax.shard_map(
        functools.partial(body, sizes=sizes),
        mesh=mesh,
        in_specs=(
            P("vel", "gx", "gy"),
            P("gx", "gy"),
            P(None, "gy"),
            P(None, "gx"),
            P("vel", None, "gy"),
            P("vel", None, "gx"),
        ),
        out_specs=P("vel", "gx", "gy"),
        check_vma=False,
    )
```

profile of v0, /device:TPU:1, one launch (start us, length us, event | category | flops | bytes accessed | tf_op | source)
XLA Modules:
  0.0 52.8 jit_solution(4953539352983318852)
XLA Ops:
  0.0 1.1 %copy.7 = bf16[1024,2,8]{2,1,0:T(2,128)(2,1)S(1)} copy(bf16[1024,2,8]{0,2,1:T(8,128)(2,1)} %param.11) | data formatting | bytes 65536 | tf_op args[5]
  1.1 0.0 copy-start
  1.1 1.6 %copy-done = bf16[1024,8,128]{2,1,0:T(8,128)(2,1)S(1)} copy-done((bf16[1024,8,128]{2,1,0:T(8,128)(2,1)S(1)}, bf16[1024,8,128]{2,1,0:T(8,128)(2,1)}, u32[]{:S(2)}) %copy-start) | copy-done | bytes 2097176
  2.7 0.0 copy-start.1
  2.7 1.0 %copy-done.1 = bf16[1024,2,128]{2,1,0:T(2,128)(2,1)S(1)} copy-done((bf16[1024,2,128]{2,1,0:T(2,128)(2,1)S(1)}, bf16[1024,2,128]{2,1,0:T(2,128)(2,1)}, u32[]{:S(2)}) %copy-start.1) | copy-done | bytes 524312
  3.7 0.0 copy-start.2
  3.7 0.7 %copy-done.2 = f32[8,128]{1,0:T(8,128)S(1)} copy-done((f32[8,128]{1,0:T(8,128)S(1)}, f32[8,128]{1,0:T(8,128)}, u32[]{:S(2)}) %copy-start.2) | copy-done | bytes 4120
  4.4 0.0 copy-start.3
  4.4 0.7 %copy-done.3 = s32[2,128]{1,0:T(2,128)S(1)} copy-done((s32[2,128]{1,0:T(2,128)S(1)}, s32[2,128]{1,0:T(2,128)}, u32[]{:S(2)}) %copy-start.3) | copy-done | bytes 1048
  5.1 0.0 copy-start.4
  5.1 0.7 %copy-done.4 = s32[2,8]{1,0:T(2,128)S(1)} copy-done((s32[2,8]{1,0:T(2,128)S(1)}, s32[2,8]{1,0:T(2,128)}, u32[]{:S(2)}) %copy-start.4) | copy-done | bytes 88
  5.8 45.7 %bgk_step.1 = bf16[8192,128]{1,0:T(8,128)(2,1)S(1)} custom-call(bf16[8192,128]{1,0:T(8,128)(2,1)S(1)} %bitcast.5, f32[8,128]{1,0:T(8,128)S(1)} %copy-done.2, s32[2,128]{1,0:T(2,128)S(1)} %copy-done.3, s32[2,8]{1,0:T(2,128)S(1)} %copy-done.4, bf16[2048,128]{1,0:T(8,128)(2,1)S(1)} %bitcast.7, bf16[2048,8]{1,0:T(8,128)(2,1)S(1)} %bitcast.6), custom_call_target="tpu_custom_call" | custom-call | tf_op jit(solution)/shard_map/bgk_step/pallas_call | solution.py:711
  51.5 1.3 %copy.9 = bf16[1024,8,128]{2,1,0:T(8,128)(2,1)} copy(bf16[1024,8,128]{2,1,0:T(8,128)(2,1)S(1)} %bitcast.4) | data formatting | bytes 4194304
Async XLA Ops:
  1.1 1.6 %copy-start = (bf16[1024,8,128]{2,1,0:T(8,128)(2,1)S(1)}, bf16[1024,8,128]{2,1,0:T(8,128)(2,1)}, u32[]{:S(2)}) copy-start(bf16[1024,8,128]{2,1,0:T(8,128)(2,1)} %param.6) | copy-start | bytes 6291460
  2.7 1.0 %copy-start.1 = (bf16[1024,2,128]{2,1,0:T(2,128)(2,1)S(1)}, bf16[1024,2,128]{2,1,0:T(2,128)(2,1)}, u32[]{:S(2)}) copy-start(bf16[1024,2,128]{2,1,0:T(2,128)(2,1)} %param.10) | copy-start | bytes 1572868
  3.7 0.7 %copy-start.2 = (f32[8,128]{1,0:T(8,128)S(1)}, f32[8,128]{1,0:T(8,128)}, u32[]{:S(2)}) copy-start(f32[8,128]{1,0:T(8,128)} %relax.1) | copy-start | bytes 12292
  4.4 0.7 %copy-start.3 = (s32[2,128]{1,0:T(2,128)S(1)}, s32[2,128]{1,0:T(2,128)}, u32[]{:S(2)}) copy-start(s32[2,128]{1,0:T(2,128)} %lrk.1) | copy-start | bytes 3076
  5.1 0.7 %copy-start.4 = (s32[2,8]{1,0:T(2,128)S(1)}, s32[2,8]{1,0:T(2,128)}, u32[]{:S(2)}) copy-start(s32[2,8]{1,0:T(2,128)} %btk.1) | copy-start | bytes 196
where the time goes:
time: 53.1 us; the launch traced here: 52.8 us
  Pallas kernels  45.7 us (86%)
  local copies, waits for them, and re-layouts  7.07 us (13%)
    pallas_call x1, Pallas kernels, body(): pl.pallas_call(functools.partial(kernel, nv, nx, ny, rows), out_shape=jax...  45.7 us
    unnamed x12, local copies, waits for them, and re-layouts  7.07 us

commit v1 on v0

--- a/solution.py
+++ b/solution.py
@@ -127,12 +127,13 @@
 
 def kernel(
     nv, nx, ny, rows,
-    prev_h, relax, lrk, btk, lri, bti,
+    prev_h, relax_h, lrk_h, btk_h, lri_h, bti_h,
     out_h,
     prev, gmain, src, afac, invd, sr, sl, rr, rl, moms, momr,
-    strip, ssrc, sinv, xg, yg, xsr, xsl, xrr, xrl, xpr, xpl, ysend, yrecv,
-    fys, fyr, fxs, fxr, inf, tmp, infs, yinf, mwy, wyt, vxl, kinds, ins, par,
-    ld, st, mom_s, mom_r, r_s, r_r, l_s, l_r, xr_s, xr_r, xl_s, xl_r,
+    strip, ssrc, sinv, yg, xsr, xsl, xrr, xrl, esrc, einv, ysend, yrecv,
+    fys, fyr, fxs, fxr, inf, infp, mwp, yinf, mwy, wyt, vxl, kinds, ins,
+    relax, lrk, btk, lri, bti,
+    ld, small, st, mom_s, mom_r, r_s, r_r, l_s, l_r, xr_s, xr_r, xl_s, xl_r,
     y_s, y_r, fy_s, fy_r, fx_s, fx_r,
 ):
     v, gx, gy = lax.axis_index("vel"), lax.axis_index("gx"), lax.axis_index("gy")
@@ -163,8 +164,16 @@
         at = pl.ds(pl.multiple_of(c * part, part), part)
         return pltpu.make_async_copy(prev_h.at[at], prev.at[at], ld.at[c])
 
+    def fetch(n):
+        pair = ((relax_h, relax), (lrk_h, lrk), (btk_h, btk), (bti_h, bti), (lri_h, lri))[n]
+        return pltpu.make_async_copy(*pair, small.at[n])
+
+    fetch(0).start()
     for c in range(CHUNKS):
         load(c).start()
+    for n in (1, 2, 3):
+        fetch(n).start()
+    pl.when(edge)(lambda: fetch(4).start())
 
     def remote(s, d, ss, rs, *dev):
         return pltpu.make_async_remote_copy(s, d, ss, rs, device_id=dev, device_id_type=MESH)
@@ -204,13 +213,6 @@
     sub = iota((8, 128), 0)
     cell = lax.rem(lane, 8)
     in_tile = lane // 8
-    irel = 1.0 / relax[...]
-
-    def inv_of(m):
-        at = pl.ds(pl.multiple_of(m * 8, 8), 8)
-        invd[at, :] = 1.0 / (DT_INV + irel + (m + 1).astype(F32) * STEP)
-
-    loop(0, NVX - 1, inv_of)
     for t in range(4):
         vxl[t * 8 : t * 8 + 8, :] = ((t * 16 + in_tile).astype(F32) - (NVX - 1) / 2.0) * STEP
     for b in range(kyn * 4 // 8):
@@ -229,8 +231,6 @@
     in_strip = posn < 4
     rep8 = (cell == sub).astype(F32)
 
-    pl.semaphore_wait(barrier, nv + not_first.astype(jnp.int32) + not_last.astype(jnp.int32))
-
     def gat(ky, off, stride=1):
         return pl.ds(ky * (NVX * PITCH) + off, 8, stride=stride)
 
@@ -245,6 +245,9 @@
     def send_chunk(s, c):
         pl.when(not_last)(lambda: halo(s, c, 0).start())
         pl.when(not_first)(lambda: halo(s, c, 1).start())
+
+    def tile(ky, t):
+        return pl.ds(pl.multiple_of(ky * 32 + t * 8, 8), 8)
 
     def take_row(ky, u):
         base = pl.multiple_of(ky * (NVX * 8), NVX * 8)
@@ -262,6 +265,9 @@
                 s1 = s1 + (a - b) * x
                 s2 = s2 + both * (x * x)
         yy = ((v * kyn + ky).astype(F32) - (NVX - 1) / 2.0) * STEP
+        got = dot_nt(sel16, prev[pl.ds(base, NVX * 8), :])
+        for t in range(4):
+            strip[tile(ky, t), :] = got[:, t * 128 : t * 128 + 128]
         pack_halo(ky, 0)
         return (u[0] + s0, u[1] + s1, u[2] + s0 * yy, u[3] + (s2 + s0 * (yy * yy)) * 0.5)
 
@@ -271,6 +277,7 @@
         send_chunk(0, c)
         return u
 
+    pl.semaphore_wait(barrier, nv + not_first.astype(jnp.int32) + not_last.astype(jnp.int32))
     zero = jnp.zeros((8, 128), F32)
     u = lax.fori_loop(0, CHUNKS, take_chunk, (zero, zero, zero, zero))
     for a in range(4):
@@ -278,36 +285,34 @@
     for k in range(1, nv):
         moment(k).start()
 
-    def take_strip(ky):
-        block = prev[pl.ds(pl.multiple_of(ky * 512, 512), 512), :]
-        got = dot_nt(sel16, block)
-        for t in range(4):
-            strip[pl.ds(pl.multiple_of(ky * 32 + t * 8, 8), 8), :] = got[:, t * 128 : t * 128 + 128]
-
-    loop(0, kyn, take_strip)
-
-    def tile(ky, t):
-        return pl.ds(pl.multiple_of(ky * 32 + t * 8, 8), 8)
-
     groups = kyn // 4
 
+    masks = [(lax.rem(iota((16, 128), 1), 8) == k).astype(F32).astype(BF16) for k in range(8)]
+
+    def pair(a, b):
+        return jnp.concatenate([a, b], axis=0).astype(BF16)
+
+    def turn(a, by):
+        return a if by % 128 == 0 else pltpu.roll(a, by % 128, 1)
+
+    def pack_strips(s, g, tiles):
+        right = left = None
+        for k in range(8):
+            r, h = k // 2, k % 2
+            c = turn(pair(tiles[0, r, 2 + h], tiles[1, r, 2 + h]), k - 7) * masks[k]
+            right = c if right is None else right + c
+            c = turn(pair(tiles[0, r, h], tiles[1, r, h]), k) * masks[k]
+            left = c if left is None else left + c
+        at = pl.ds(pl.multiple_of(g * 16, 16), 16)
+        xsr[s, at, :] = right
+        xsl[s, at, :] = left
+
+    def pack_first(g):
+        pack_strips(
+            0, g, {(n, r, t): strip[tile((g * 2 + n) * 4 + r, t), :] for n in range(2) for r in range(4) for t in range(4)}
+        )
+
     def send_strips(s):
-        def pack(g):
-            right = left = jnp.zeros((8, 128), F32)
-            for r in range(4):
-                for h in range(2):
-                    k = r * 2 + h
-                    c = strip[tile(g * 4 + r, 2 + h), :]
-                    right = jnp.where(cell == k, c if k == 7 else pltpu.roll(c, (k - 7) % 128, 1), right)
-                    c = strip[tile(g * 4 + r, h), :]
-                    left = jnp.where(cell == k, c if k == 0 else pltpu.roll(c, k, 1), left)
-            at = pl.ds(pl.multiple_of(g * 8, 8), 8)
-            xpr[at, :] = right
-            xpl[at, :] = left
-
-        loop(0, groups, pack)
-        xsr[s] = xpr[...].astype(BF16)
-        xsl[s] = xpl[...].astype(BF16)
         pl.when(not_last)(lambda: shalo(s, 0).start())
         pl.when(not_first)(lambda: shalo(s, 1).start())
 
@@ -330,22 +335,30 @@
             for k in range(half):
                 fluxy(s, k).start()
 
+    def speed_rows(q, positive):
+        j = (q * 8 + sub).astype(F32)
+        return (j + 0.5) * STEP if positive else (HALF - 0.5 - j) * STEP
+
     def send_edges(s):
         def partial(rows_ref, tile_off, spot):
-            def add(ky, carry):
-                main, thin = carry
-                block = rows_ref[s, pl.ds(pl.multiple_of(ky * HALF, HALF), HALF), :].astype(F32)
-                for q in range(HALF // 8):
-                    j = (q * 8 + sub).astype(F32)
-                    x = (j + 0.5) * STEP if tile_off else (HALF - 0.5 - j) * STEP
-                    main = main + block[q * 8 : q * 8 + 8] * x
-                for h in range(2):
-                    c = strip[tile(ky, tile_off + h), :]
-                    x = jnp.abs(vxl[(tile_off + h) * 8 : (tile_off + h) * 8 + 8, :])
-                    thin = thin + c * jnp.where(cell == spot, x, 0.0)
-                return main, thin
-
-            main, thin = lax.fori_loop(0, kyn, add, (zero, zero))
+            def add(g, carry):
+                main, thin = list(carry[:4]), list(carry[4:])
+                for r in range(4):
+                    ky = g * 4 + r
+                    block = rows_ref[s, pl.ds(pl.multiple_of(ky * HALF, HALF), HALF), :].astype(F32)
+                    for q in range(HALF // 8):
+                        main[q] = main[q] + block[q * 8 : q * 8 + 8]
+                    for h in range(2):
+                        thin[h] = thin[h] + strip[tile(ky, tile_off + h), :]
+                return (*main, *thin)
+
+            got = lax.fori_loop(0, groups, add, (zero,) * 6)
+            main = thin = zero
+            for q in range(HALF // 8):
+                main = main + got[q] * speed_rows(q, tile_off > 0)
+            for h in range(2):
+                x = jnp.abs(vxl[(tile_off + h) * 8 : (tile_off + h) * 8 + 8, :])
+                thin = thin + got[4 + h] * jnp.where(cell == spot, x, 0.0)
             thin = jnp.broadcast_to(jnp.sum(thin, axis=1, keepdims=True), (8, 128)) * sel_up
             fxs[s] = (jnp.where(in_strip, 0.0, main) + thin) * FLUX_SCALE
             for k in range(1, nv):
@@ -354,50 +367,72 @@
         pl.when(first)(lambda: partial(sl, 0, 0))
         pl.when(last)(lambda: partial(sr, 2, 7))
 
+    loop(0, groups // 2, pack_first)
     send_strips(0)
     send_edges(0)
 
+    fetch(0).wait()
+    irel = 1.0 / relax[...]
+    base_inv = DT_INV + irel
+
+    def inv_of(m):
+        for d in range(7):
+            at = pl.ds(pl.multiple_of(m * 56 + d * 8, 8), 8)
+            invd[at, :] = 1.0 / (base_inv + (m * 7 + (d + 1)).astype(F32) * STEP)
+
+    loop(0, (NVX - 1) // 7, inv_of)
+
+    permute = (iota((128, 128), 0) == lax.rem(iota((128, 128), 1), 8) * 16 + iota((128, 128), 1) // 8).astype(F32)
+    fetch(1).wait()
+    fetch(2).wait()
+    fetch(3).wait()
+
     @pl.when(edge)
     def _():
+        fetch(4).wait()
         side = jnp.where(first, 0, 1)
         off = jnp.where(first, HALF, 0)
-
-        def take(ky):
-            at = pl.ds(pl.multiple_of((ky * NVX + off) * 2, 2 * HALF), 2 * HALF)
-            tmp[...] = lri[at, :].astype(F32)
-            for q in range(HALF // 8):
-                at = pl.ds(pl.multiple_of(ky * HALF + q * 8, 8), 8)
-                inf[at, :] = tmp[pl.ds(q * 16 + side, 8, stride=2), :]
-
-        loop(0, kyn, take)
-        kind = jnp.where(first, lrk[0:1, :], lrk[1:2, :]).astype(F32)
-        kinds[0:8, :] = jnp.broadcast_to(kind, (8, 128))
-        kinds[8:16, :] = dot_nt(sel, jnp.broadcast_to(kind, (128, 128)))
-
-        def spread(b):
-            got = dot_nt(sel, inf[pl.ds(pl.multiple_of(b * 128, 128), 128), :])
-            for w in range(8):
-                rep = (iota((128, 128), 0) == w * 16 + iota((128, 128), 1) // 8).astype(F32)
-                infs[pl.ds(pl.multiple_of(b * 64 + w * 8, 8), 8), :] = jnp.dot(got, rep, preferred_element_type=F32)
-
-        loop(0, kyn * HALF // 128, spread)
+        kind = jnp.broadcast_to(jnp.where(first, lrk[0:1, :], lrk[1:2, :]).astype(F32), (8, 128))
+        kinds[0:8, :] = 1.0 - kind
+        kind8 = jnp.broadcast_to(jnp.sum(kind * sel, axis=1, keepdims=True), (8, 128))
+        kinds[8:16, :] = 1.0 - kind8
+
+        def take(g):
+            for r in range(4):
+                ky = g * 4 + r
+                at = pl.ds(pl.multiple_of((ky * NVX + off) * 2, 2 * HALF), 2 * HALF)
+                src[pl.ds(pl.multiple_of(ky * 2 * HALF, 2 * HALF), 2 * HALF), :] = lri[at, :].astype(F32)
+            for r in range(4):
+                ky = g * 4 + r
+                for q in range(HALF // 8):
+                    at = pl.ds(pl.multiple_of(ky * HALF + q * 8, 8), 8)
+                    inf[at, :] = src[pl.ds(ky * 2 * HALF + q * 16 + side, 8, stride=2), :]
+            got = dot_nt(sel, inf[pl.ds(pl.multiple_of(g * 128, 128), 128), :])
+            at = pl.ds(pl.multiple_of(g * 8, 8), 8)
+            infp[at, :] = kind8 * jnp.dot(got, permute, preferred_element_type=F32)
+            kyg = (v * kyn + g * 4 + cell // 2).astype(F32)
+            kxg = (off // 16 * 16 + lax.rem(cell, 2) * 16 + in_tile).astype(F32)
+            yy, xx = (kyg - (NVX - 1) / 2.0) * STEP, (kxg - (NVX - 1) / 2.0) * STEP
+            mwp[at, :] = jnp.exp((xx * xx + yy * yy) * -0.5)
+            for q in range(16):
+                at = pl.ds(pl.multiple_of(g * 128 + q * 8, 8), 8)
+                inf[at, :] = inf[at, :] * kind
+
+        loop(0, groups, take)
 
     @pl.when(upwind)
     def _():
-        side = jnp.where(up, 0, 1)
-        row = iota((512, 128), 0)
-        keep = jnp.logical_and(lax.rem(row, 2) == side, lax.rem(row // 2, 16) == iota((512, 128), 1) // 8)
-        gather = (iota((16, 512), 1) // 32 == iota((16, 512), 0)).astype(F32)
-
-        def take(b):
-            block = bti[pl.ds(pl.multiple_of(b * 512, 512), 512), :].astype(F32)
-            wide = jnp.dot(block, rep8, preferred_element_type=F32)
-            wide = jnp.where(keep, wide, 0.0)
-            yinf[pl.ds(pl.multiple_of(b * 16, 16), 16), :] = jnp.dot(gather, wide, preferred_element_type=F32)
-
-        loop(0, rows * 2 // 512, take)
-        kind = jnp.where(up, btk[0:1, :], btk[1:2, :]).astype(F32)
-        kinds[16:24, :] = jnp.dot(jnp.broadcast_to(kind, (8, 8)), rep8, preferred_element_type=F32)
+        block = jnp.where(up, bti[0].astype(F32), bti[1].astype(F32))
+        stack = jnp.concatenate([block[:, b * 128 : b * 128 + 128] for b in range(rows // 128)], axis=0)
+        kind = jnp.broadcast_to(jnp.where(up, btk[0:1, :], btk[1:2, :]).astype(F32), (8, 8))
+        kind = jnp.dot(kind, rep8, preferred_element_type=F32)
+        kinds[16:24, :] = 1.0 - kind
+        for w in range(8):
+            spread = (iota((128, 128), 0) == w * 16 + iota((128, 128), 1) // 8).astype(F32)
+            wide = jnp.dot(stack, spread, preferred_element_type=F32)
+            for b in range(rows // 128):
+                one = jnp.where(cell == sub, wide[b * 8 : b * 8 + 8], 0.0) * kind
+                yinf[b * 8 + w : b * 8 + w + 1, :] = jnp.sum(one, axis=0, keepdims=True)
 
     for k in range(1, nv):
         moment(k).wait_recv()
@@ -432,45 +467,21 @@
         return jnp.broadcast_to(jnp.sum(total, axis=0, keepdims=True), (8, 128))
 
     def sweep_strips(s):
-        @pl.when(not_first)
-        def _():
-            shalo(s, 0).wait_recv()
-            xpr[...] = xrr[s].astype(F32)
-
-            def put(g):
-                c = xpr[pl.ds(pl.multiple_of(g * 8, 8), 8), :]
-                for k in range(8):
-                    xg[tile(g * 4 + k // 2, 2 + k % 2), :] = c if k == 0 else pltpu.roll(c, 128 - k, 1)
-
-            loop(0, groups, put)
-
-        @pl.when(not_last)
-        def _():
-            shalo(s, 1).wait_recv()
-            xpl[...] = xrl[s].astype(F32)
-
-            def put(g):
-                c = xpl[pl.ds(pl.multiple_of(g * 8, 8), 8), :]
-                for k in range(8):
-                    xg[tile(g * 4 + k // 2, k % 2), :] = c if k == 7 else pltpu.roll(c, 7 - k, 1)
-
-            loop(0, groups, put)
+        pl.when(not_first)(lambda: shalo(s, 0).wait_recv())
+        pl.when(not_last)(lambda: shalo(s, 1).wait_recv())
 
         @pl.when(edge)
         def _():
             for k in range(1, nv):
                 fluxx(s, k).wait_recv()
-            kind = kinds[8:16, :]
-            flux = jnp.broadcast_to(jnp.sum(edge_flux(s) * sel, axis=1, keepdims=True), (8, 128)) * (1.0 - kind)
-
-            def fill(ky, t0):
-                for h in range(2):
-                    wall = mwy[pl.ds(ky * 4 + t0 + h, 1), :]
-                    inflow = infs[pl.ds(pl.multiple_of(ky * 16 + h * 8, 8), 8), :]
-                    xg[tile(ky, t0 + h), :] = kind * inflow + flux * wall
-
-            pl.when(first)(lambda: loop(0, kyn, lambda ky: fill(ky, 2)))
-            pl.when(last)(lambda: loop(0, kyn, lambda ky: fill(ky, 0)))
+            flux = jnp.broadcast_to(jnp.sum(edge_flux(s) * sel, axis=1, keepdims=True), (8, 128)) * kinds[8:16, :]
+
+            def fill(ref):
+                ghost = [infp[g * 8 : g * 8 + 8, :] + flux * mwp[g * 8 : g * 8 + 8, :] for g in range(groups)]
+                ref[s] = jnp.concatenate(ghost, axis=0).astype(BF16)
+
+            pl.when(first)(lambda: fill(xrr))
+            pl.when(last)(lambda: fill(xrl))
 
         @pl.when(downwind)
         def _():
@@ -487,82 +498,142 @@
             flux = jnp.broadcast_to(jnp.sum(total, axis=0, keepdims=True), (8, 128))
             for k in (8, 16, 32, 64):
                 flux = flux + pltpu.roll(flux, k, 1)
-            kind = kinds[16:24, :]
-            flux = flux * (1.0 - kind)
+            flux = flux * kinds[16:24, :]
             for b in range(kyn * 4 // 8):
                 at = slice(b * 8, b * 8 + 8)
-                yg[at, :] = kind * yinf[at, :] + flux * mwy[at, :]
-
-        def step(ky):
-            yy = speed_y(ky)
-            ay = jnp.abs(yy)
-            for t in range(4):
-                c = strip[tile(ky, t), :]
-                xx = vxl[t * 8 : t * 8 + 8, :]
-                ax = jnp.abs(xx)
+                yg[at, :] = yinf[at, :] + flux * mwy[at, :]
+
+        def step(g):
+            at = pl.ds(pl.multiple_of(g * 16, 16), 16)
+            right, left = xrr[s, at, :], xrl[s, at, :]
+            tiles = {}
+            for r in range(4):
+                for t in range(4):
+                    old = [strip[tile((g * 2 + n) * 4 + r, t), :] for n in range(2)]
+                    moved = turn(pair(*old), 1 if t >= 2 else -1).astype(F32)
+                    k = r * 2 + t % 2
+                    ghost = (turn(right, -k) if t >= 2 else turn(left, 7 - k)).astype(F32)
+                    hole = cell == (0 if t >= 2 else 7)
+                    xx = vxl[t * 8 : t * 8 + 8, :]
+                    ax = jnp.abs(xx)
+                    for n in range(2):
+                        ky = (g * 2 + n) * 4 + r
+                        yy = speed_y(ky)
+                        ay = jnp.abs(yy)
+                        c = old[n]
+                        if s == 0:
+                            power = thin[0] + xx * thin[1] + yy * thin[2] + (xx * xx + yy * yy) * 0.5 * thin[3]
+                            source = c * DT_INV + jnp.exp(power) * thin[4]
+                            inv = 1.0 / (DT_INV + thin[4] + ax + ay)
+                            ssrc[tile(ky, t), :] = source
+                            sinv[tile(ky, t), :] = inv
+                        else:
+                            source = ssrc[tile(ky, t), :]
+                            inv = sinv[tile(ky, t), :]
+                        from_y = jnp.where(sub == 0, yg[pl.ds(ky * 4 + t, 1), :], pltpu.roll(c, 1, 0))
+                        from_x = jnp.where(hole, ghost[n * 8 : n * 8 + 8], moved[n * 8 : n * 8 + 8])
+                        new = (source + ax * from_x + ay * from_y) * inv
+                        tiles[n, r, t] = new
+            for (n, r, t), new in tiles.items():
+                strip[tile((g * 2 + n) * 4 + r, t), :] = new
+            if s < SWEEPS - 1:
+                pack_strips(s + 1, g, tiles)
+
+        loop(0, groups // 2, step)
+
+    def next_edges(s):
+        off = jnp.where(first, 0, PITCH * HALF + 8)
+        beside = jnp.where(first, 1, -1)
+        kx0 = jnp.where(first, 0, HALF)
+        row = jnp.where(first, 0, 7)
+        speeds = [jnp.where(first, speed_rows(q, False), speed_rows(q, True)) for q in range(HALF // 8)]
+        pick = (sub == row).astype(F32)
+
+        def row_of(a):
+            return jnp.broadcast_to(jnp.sum(a * pick, axis=0, keepdims=True), (8, 128))
+
+        inv_row = row_of(base_inv) if s == 0 else None
+
+        def add(g, carry):
+            main = list(carry[:4])
+            thin_sum = list(carry[4:])
+            for r in range(4):
+                ky = g * 4 + r
+                yy = speed_y(ky)
+                ay = jnp.abs(yy)
                 if s == 0:
-                    power = thin[0] + xx * thin[1] + yy * thin[2] + (xx * xx + yy * yy) * 0.5 * thin[3]
-                    source = c * DT_INV + jnp.exp(power) * thin[4]
-                    inv = 1.0 / (DT_INV + thin[4] + ax + ay)
-                    ssrc[tile(ky, t), :] = source
-                    sinv[tile(ky, t), :] = inv
-                else:
-                    source = ssrc[tile(ky, t), :]
-                    inv = sinv[tile(ky, t), :]
-                from_y = jnp.where(sub == 0, yg[pl.ds(ky * 4 + t, 1), :], pltpu.roll(c, 1, 0))
-                if t >= 2:
-                    from_x = jnp.where(cell == 0, xg[tile(ky, t), :], pltpu.roll(c, 1, 1))
-                else:
-                    from_x = jnp.where(cell == 7, xg[tile(ky, t), :], pltpu.roll(c, 127, 1))
-                strip[tile(ky, t), :] = (source + ax * from_x + ay * from_y) * inv
-
-        loop(0, kyn, step)
+                    bfac = row_of(b_of(yy))
+                for q in range(0, HALF // 8, 2):
+                    own = [gmain[gat(ky, off + PITCH * 8 * (q + d), PITCH), :] for d in range(2)]
+                    turned = pltpu.roll(pair(*own), roll_by, 1).astype(F32)
+                    for d in range(2):
+                        moved = gmain[gat(ky, off + beside + PITCH * 8 * (q + d), PITCH), :]
+                        at = pl.ds(pl.multiple_of(ky * HALF + (q + d) * 8, 8), 8)
+                        ax = speeds[q + d]
+                        if s == 0:
+                            fac = afac[pl.ds((kx0 + 8 * (q + d)) * 8 + row, 8, stride=8), :]
+                            source = own[d] * DT_INV + fac * bfac
+                            inv = 1.0 / (inv_row + ax + ay)
+                            esrc[at, :] = source
+                            einv[at, :] = inv
+                        else:
+                            source = esrc[at, :]
+                            inv = einv[at, :]
+                        new = (source + ax * moved + ay * turned[d * 8 : d * 8 + 8]) * inv
+                        main[q + d] = main[q + d] + new
+                for h in range(2):
+                    thin_sum[h] = thin_sum[h] + strip[tile(ky, kx0 // 16 + h), :]
+            return (*main, *thin_sum)
+
+        got = lax.fori_loop(0, groups, add, (zero,) * 6)
+        main = thin = zero
+        for q in range(HALF // 8):
+            main = main + got[q] * speeds[q]
+        for h in range(2):
+            x = jnp.abs(vxl[pl.ds(pl.multiple_of((kx0 // 16 + h) * 8, 8), 8), :])
+            thin = thin + got[4 + h] * jnp.where(cell == row, x, 0.0)
+        thin = jnp.broadcast_to(jnp.sum(thin, axis=1, keepdims=True), (8, 128)) * sel_up
+        fxs[s + 1] = (jnp.where(in_strip, 0.0, main) + thin) * FLUX_SCALE
+        for k in range(1, nv):
+            fluxx(s + 1, k).start()
 
     def fill_main(s, c):
+        def put(ref, off):
+            for r in range(per):
+                ky = c * per + r
+                block = ref[s, pl.ds(pl.multiple_of(ky * HALF, HALF), HALF), :].astype(F32)
+                for q in range(HALF // 8):
+                    gmain[gat(ky, off + PITCH * 8 * q, PITCH), :] = block[q * 8 : q * 8 + 8]
+
         @pl.when(not_first)
         def _():
             halo(s, c, 0).wait_recv()
-
-            def put(ky):
-                block = rr[s, pl.ds(pl.multiple_of(ky * HALF, HALF), HALF), :].astype(F32)
+            put(rr, PITCH * HALF)
+
+        @pl.when(not_last)
+        def _():
+            halo(s, c, 1).wait_recv()
+            put(rl, 8)
+
+        @pl.when(edge)
+        def _():
+            flux = edge_flux(s) * kinds[0:8, :]
+
+            def put_wall(positive, off):
+                walls = []
                 for q in range(HALF // 8):
-                    gmain[gat(ky, PITCH * (HALF + 8 * q), PITCH), :] = block[q * 8 : q * 8 + 8]
-
-            loop(c * per, c * per + per, put)
-
-        @pl.when(not_last)
-        def _():
-            halo(s, c, 1).wait_recv()
-
-            def put(ky):
-                block = rl[s, pl.ds(pl.multiple_of(ky * HALF, HALF), HALF), :].astype(F32)
-                for q in range(HALF // 8):
-                    gmain[gat(ky, PITCH * 8 * q + 8, PITCH), :] = block[q * 8 : q * 8 + 8]
-
-            loop(c * per, c * per + per, put)
-
-        @pl.when(edge)
-        def _():
-            kind = kinds[0:8, :]
-            flux = edge_flux(s) * (1.0 - kind)
-
-            def rows_of(ky, q, positive):
-                j = (q * 8 + sub).astype(F32)
-                x = (j + 0.5) * STEP if positive else (HALF - 0.5 - j) * STEP
-                yy = speed_y(ky)
-                wall = jnp.exp((x * x + yy * yy) * -0.5)
-                return kind * inf[pl.ds(pl.multiple_of(ky * HALF + q * 8, 8), 8), :] + flux * wall
-
-            def put_low(ky):
-                for q in range(HALF // 8):
-                    gmain[gat(ky, PITCH * (HALF + 8 * q), PITCH), :] = rows_of(ky, q, True)
-
-            def put_high(ky):
-                for q in range(HALF // 8):
-                    gmain[gat(ky, PITCH * 8 * q + 8, PITCH), :] = rows_of(ky, q, False)
-
-            pl.when(first)(lambda: loop(c * per, c * per + per, put_low))
-            pl.when(last)(lambda: loop(c * per, c * per + per, put_high))
+                    x = speed_rows(q, positive)
+                    walls.append(flux * jnp.exp(x * x * -0.5))
+                for r in range(per):
+                    ky = c * per + r
+                    yy = speed_y(ky)
+                    scale = jnp.exp(jnp.full((8, 128), yy * yy * -0.5))
+                    for q in range(HALF // 8):
+                        brought = inf[pl.ds(pl.multiple_of(ky * HALF + q * 8, 8), 8), :]
+                        gmain[gat(ky, off + PITCH * 8 * q, PITCH), :] = brought + walls[q] * scale
+
+            pl.when(first)(lambda: put_wall(True, PITCH * HALF))
+            pl.when(last)(lambda: put_wall(False, 8))
 
     def main_row(ky, s, b_of):
         yy = speed_y(ky)
@@ -574,21 +645,29 @@
             bfac = b_of(yy)
         for i in range(0, HALF, 2):
             inv = [invd[pl.ds(pl.multiple_of((jj + i + d) * 8, 8), 8), :] for d in range(2)]
+            owns = {}
+            for positive in (True, False):
+                for d in range(2):
+                    kx = HALF + i + d if positive else HALF - 1 - i - d
+                    owns[positive, d] = gmain[gat(ky, PITCH * kx + (1 if positive else 0)), :]
+            turned = {}
+            for positive in (True, False):
+                pair = jnp.concatenate([owns[positive, d] for d in range(2)], axis=0).astype(BF16)
+                turned[positive] = pltpu.roll(pair, roll_by, 1).astype(F32)
             for positive in (True, False):
                 done = []
                 for d in range(2):
                     kx = HALF + i + d if positive else HALF - 1 - i - d
                     own_off = PITCH * kx + (1 if positive else 0)
-                    own = gmain[gat(ky, own_off), :]
                     moved = gmain[gat(ky, PITCH * kx + (0 if positive else 1)), :]
-                    turned = pltpu.roll(own, roll_by, 1)
                     at = pl.ds(base + kx * 8, 8)
                     if s == 0:
-                        source = own * DT_INV + afac[kx * 8 : kx * 8 + 8, :] * bfac
+                        source = owns[positive, d] * DT_INV + afac[kx * 8 : kx * 8 + 8, :] * bfac
                         src[at, :] = source
                     else:
                         source = src[at, :]
-                    new = (source + moved * ABS[i + d] + turned * ay) * inv[d]
+                    beside = turned[positive][d * 8 : d * 8 + 8]
+                    new = (source + moved * ABS[i + d] + beside * ay) * inv[d]
                     if s < SWEEPS - 1:
                         gmain[gat(ky, own_off), :] = new
                     else:
@@ -599,6 +678,14 @@
                         done = done[::-1]
                     prev[pl.ds(base + kx * 8, 16), :] = jnp.concatenate(done, axis=0).astype(BF16)
 
+    def place(t):
+        row = iota((128, 128), 0)
+        hit = jnp.logical_and(row // 8 == t, lax.rem(row, 8) < 4)
+        there = jnp.where(up, iota((128, 128), 1), 127 - iota((128, 128), 1))
+        return jnp.logical_and(hit, there == lax.rem(row, 8)).astype(BF16)
+
+    back = [place(t) for t in range(16)]
+
     def store(c):
         at = pl.ds(pl.multiple_of(c * part, part), part)
         return pltpu.make_async_copy(prev.at[at], out_h.at[at], st.at[c])
@@ -617,14 +704,16 @@
         sweep_strips(s)
         if s < SWEEPS - 1:
             send_strips(s + 1)
+            pl.when(edge)(lambda: next_edges(s))
         else:
 
-            def put(ky):
-                for t in range(4):
-                    at = pl.ds(pl.multiple_of(ky * 512 + t * 128, 128), 128)
-                    ins[at, :] = dot_tn(strip[tile(ky, t), :], sel_up)
-
-            loop(0, kyn, put)
+            def put(g):
+                flat = strip[pl.ds(pl.multiple_of(g * 128, 128), 128), :].T.astype(BF16)
+                for t in range(16):
+                    at = pl.ds(pl.multiple_of(g * 2048 + t * 128, 128), 128)
+                    ins[at, :] = jnp.dot(flat, back[t], preferred_element_type=F32)
+
+            loop(0, groups, put)
 
         def chunk(c):
             fill_main(s, c)
@@ -641,8 +730,6 @@
                 store(c).start()
 
         loop(0, CHUNKS, chunk)
-        if s < SWEEPS - 1:
-            send_edges(s + 1)
 
     for k in range(1, nv):
         moment(k).wait_send()
@@ -689,33 +776,34 @@
         vm((SWEEPS, hr, 128), BF16), vm((SWEEPS, hr, 128), BF16),
         vm((SWEEPS, hr, 128), BF16), vm((SWEEPS, hr, 128), BF16),
         vm((32, 128), F32), vm((nv - 1, 32, 128), F32),
-        vm((thin, 128), F32), vm((thin, 128), F32), vm((thin, 128), F32), vm((thin, 128), F32),
+        vm((thin, 128), F32), vm((thin, 128), F32), vm((thin, 128), F32),
         vm((ur, 128), F32),
         vm((SWEEPS, xr, 128), BF16), vm((SWEEPS, xr, 128), BF16),
         vm((SWEEPS, xr, 128), BF16), vm((SWEEPS, xr, 128), BF16),
-        vm((xr, 128), F32), vm((xr, 128), F32),
+        vm((hr, 128), F32), vm((hr, 128), F32),
         vm((SWEEPS, ur, 128), BF16), vm((SWEEPS, ur, 128), BF16),
         vm((SWEEPS, 8, 128), F32), vm((SWEEPS, nv // 2, 8, 128), F32),
         vm((SWEEPS, 8, 128), F32), vm((SWEEPS, nv - 1, 8, 128), F32),
-        vm((hr, 128), F32), vm((NVX, 128), F32), vm((thin // 2, 128), F32),
+        vm((hr, 128), F32), vm((xr, 128), F32), vm((xr, 128), F32),
         vm((ur, 128), F32), vm((ur, 128), F32), vm((ur, 128), F32),
-        vm((32, 128), F32), vm((24, 128), F32), vm((rows * 8, 128), F32), vm((8, 128), F32),
-        dma((CHUNKS,)), dma((CHUNKS,)), dma((nv - 1,)), dma((nv - 1,)),
+        vm((32, 128), F32), vm((24, 128), F32), vm((rows * 8, 128), F32),
+        vm((8, 128), F32), vm((2, 128), jnp.int32), vm((2, 8), jnp.int32),
+        vm((rows * 2, 128), BF16), vm((2, 8, rows), BF16),
+        dma((CHUNKS,)), dma((5,)), dma((CHUNKS,)), dma((nv - 1,)), dma((nv - 1,)),
         dma((SWEEPS, CHUNKS)), dma((SWEEPS, CHUNKS)), dma((SWEEPS, CHUNKS)), dma((SWEEPS, CHUNKS)),
         dma((SWEEPS,)), dma((SWEEPS,)), dma((SWEEPS,)), dma((SWEEPS,)),
         dma((SWEEPS,)), dma((SWEEPS,)), dma((SWEEPS, nv // 2)), dma((SWEEPS, nv // 2)),
         dma((SWEEPS, nv - 1)), dma((SWEEPS, nv - 1)),
     ]
-    whole = pl.BlockSpec(memory_space=pltpu.VMEM)
     far = pl.BlockSpec(memory_space=pl.ANY)
     out = pl.pallas_call(
         functools.partial(kernel, nv, nx, ny, rows),
         out_shape=jax.ShapeDtypeStruct((rows * 8, 128), BF16),
-        in_specs=[far, whole, whole, whole, whole, whole],
+        in_specs=[far] * 6,
         out_specs=far,
         scratch_shapes=scratch,
         compiler_params=pltpu.CompilerParams(
-            collective_id=0, has_side_effects=True, vmem_limit_bytes=48 * 1024 * 1024
+            collective_id=0, has_side_effects=True, vmem_limit_bytes=62 * 1024 * 1024
         ),
         name="bgk_step",
     )(
@@ -724,7 +812,7 @@
         left_right_kind,
         bottom_top_kind,
         left_right_inflow.reshape(rows * 2, 128),
-        bottom_top_inflow.reshape(rows * 2, 8),
+        bottom_top_inflow.transpose(1, 2, 0),
     )
     return out.reshape(rows, cx, cy)
 

time: 53.1 us -> 32.6 us (0.61)
  the two profiles are of different devices: /device:TPU:1 before, /device:TPU:96 now
where the time goes in v1:
time: 32.6 us; the launch traced here: 32.4 us
  Pallas kernels  29.4 us (90%)
  local copies, waits for them, and re-layouts  3.05 us (9%)
    pallas_call x1, Pallas kernels, body(): pl.pallas_call(functools.partial(kernel, nv, nx, ny, rows), out_shape=jax...  29.4 us
    unnamed x1, local copies, waits for them, and re-layouts  3.05 us

profile of v1, /device:TPU:96, one launch (start us, length us, event | category | flops | bytes accessed | tf_op | source)
XLA Modules:
  0.0 32.4 jit_solution(53451781418615770)
XLA Ops:
  0.0 29.4 %bgk_step.1 = bf16[8192,128]{1,0:T(8,128)(2,1)} custom-call(bf16[8192,128]{1,0:T(8,128)(2,1)} %bitcast.5, f32[8,128]{1,0:T(8,128)} %relax_h.1, s32[2,128]{1,0:T(2,128)} %lrk_h.1, s32[2,8]{1,0:T(2,128)} %btk_h.1, bf16[2048,128]{1,0:T(8,128)(2,1)} %bitcast.6, bf16[2,8,1024]{2,1,0:T(8,128)(2,1)} %bitcast.7), custom_call_target="tpu_custom_call" | custom-call | tf_op jit(solution)/shard_map/bgk_step/pallas_call | solution.py:799
  29.4 3.0 %copy.8 = bf16[1024,8,128]{2,1,0:T(8,128)(2,1)} copy(bf16[1024,8,128]{2,1,0:T(8,128)(2,1)} %bitcast.4) | data formatting | bytes 4194304

commit v2 on v1

--- a/solution.py
+++ b/solution.py
@@ -131,7 +131,7 @@
     out_h,
     prev, gmain, src, afac, invd, sr, sl, rr, rl, moms, momr,
     strip, ssrc, sinv, yg, xsr, xsl, xrr, xrl, esrc, einv, ysend, yrecv,
-    fys, fyr, fxs, fxr, inf, infp, mwp, yinf, mwy, wyt, vxl, kinds, ins,
+    fys, fyr, fxs, fxr, inf, infp, mwp, yinf, mwy, wyt, vxl, kinds, ins, flat, back,
     relax, lrk, btk, lri, bti,
     ld, small, st, mom_s, mom_r, r_s, r_r, l_s, l_r, xr_s, xr_r, xl_s, xl_r,
     y_s, y_r, fy_s, fy_r, fx_s, fx_r,
@@ -265,25 +265,28 @@
                 s1 = s1 + (a - b) * x
                 s2 = s2 + both * (x * x)
         yy = ((v * kyn + ky).astype(F32) - (NVX - 1) / 2.0) * STEP
-        got = dot_nt(sel16, prev[pl.ds(base, NVX * 8), :])
-        for t in range(4):
-            strip[tile(ky, t), :] = got[:, t * 128 : t * 128 + 128]
-        pack_halo(ky, 0)
         return (u[0] + s0, u[1] + s1, u[2] + s0 * yy, u[3] + (s2 + s0 * (yy * yy)) * 0.5)
 
     def take_chunk(c, u):
         load(c).wait()
-        u = lax.fori_loop(c * per, c * per + per, take_row, u)
-        send_chunk(0, c)
-        return u
-
-    pl.semaphore_wait(barrier, nv + not_first.astype(jnp.int32) + not_last.astype(jnp.int32))
+        return lax.fori_loop(c * per, c * per + per, take_row, u)
+
     zero = jnp.zeros((8, 128), F32)
     u = lax.fori_loop(0, CHUNKS, take_chunk, (zero, zero, zero, zero))
     for a in range(4):
         moms[a * 8 : a * 8 + 8, :] = u[a] * WEIGHT
+    pl.semaphore_wait(barrier, nv + not_first.astype(jnp.int32) + not_last.astype(jnp.int32))
     for k in range(1, nv):
         moment(k).start()
+
+    def take_strip(g):
+        for r in range(4):
+            ky = g * 4 + r
+            got = dot_nt(sel16, prev[pl.ds(pl.multiple_of(ky * (NVX * 8), NVX * 8), NVX * 8), :])
+            for t in range(4):
+                strip[tile(ky, t), :] = got[:, t * 128 : t * 128 + 128]
+
+    loop(0, kyn // 4, take_strip)
 
     groups = kyn // 4
 
@@ -369,6 +372,13 @@
 
     loop(0, groups // 2, pack_first)
     send_strips(0)
+
+    def first_halo(c):
+        for r in range(per):
+            pack_halo(c * per + r, 0)
+        send_chunk(0, c)
+
+    loop(0, CHUNKS, first_halo)
     send_edges(0)
 
     fetch(0).wait()
@@ -381,6 +391,14 @@
             invd[at, :] = 1.0 / (base_inv + (m * 7 + (d + 1)).astype(F32) * STEP)
 
     loop(0, (NVX - 1) // 7, inv_of)
+
+    def place(t):
+        row, col = iota((128, 128), 0), iota((128, 128), 1)
+        there = jnp.where(up, col, 127 - col)
+        hit = jnp.logical_and(row == t * 8 + there, there < 4)
+        back[pl.ds(pl.multiple_of(t * 128, 128), 128), :] = hit.astype(F32).astype(BF16)
+
+    loop(0, 16, place)
 
     permute = (iota((128, 128), 0) == lax.rem(iota((128, 128), 1), 8) * 16 + iota((128, 128), 1) // 8).astype(F32)
     fetch(1).wait()
@@ -452,10 +470,23 @@
             afac[(HALF - 1 - j) * 8 : (HALF - j) * 8, :] = minus
     height = p[0] + top_x
 
-    thin = [
-        dot_nt(sel, jnp.broadcast_to(a[None], (16, 8, 128)).reshape(128, 128), precision=lax.Precision.HIGHEST)
-        for a in (*p, irel)
-    ]
+    def three(a):
+        high = a.astype(BF16)
+        rest = a - high.astype(F32)
+        mid = rest.astype(BF16)
+        low = (rest - mid.astype(F32)).astype(BF16)
+        return high, mid, low
+
+    def eightfold(a):
+        twice = jnp.concatenate([a, a], axis=0)
+        return jnp.concatenate([twice] * 8, axis=0)
+
+    split = [three(a) for a in (*p, irel)]
+    wide = jnp.concatenate(
+        [jnp.concatenate([eightfold(part[n]) for part in split], axis=0) for n in range(3)], axis=1
+    )
+    wide = dot_nt(jnp.concatenate([sel16] * 3, axis=1), wide)
+    thin = [wide[:, a * 128 : a * 128 + 128] for a in range(5)]
 
     def speed_y(ky):
         return ((v * kyn + ky).astype(F32) - (NVX - 1) / 2.0) * STEP
@@ -678,13 +709,12 @@
                         done = done[::-1]
                     prev[pl.ds(base + kx * 8, 16), :] = jnp.concatenate(done, axis=0).astype(BF16)
 
-    def place(t):
-        row = iota((128, 128), 0)
-        hit = jnp.logical_and(row // 8 == t, lax.rem(row, 8) < 4)
-        there = jnp.where(up, iota((128, 128), 1), 127 - iota((128, 128), 1))
-        return jnp.logical_and(hit, there == lax.rem(row, 8)).astype(BF16)
-
-    back = [place(t) for t in range(16)]
+    def bring_back(ky):
+        these = flat[pl.ds(pl.multiple_of(ky // 4 * 128, 128), 128), :]
+        for t in range(4):
+            at = pl.ds(pl.multiple_of(ky * 512 + t * 128, 128), 128)
+            weights = back[pl.ds(pl.multiple_of((lax.rem(ky, 4) * 4 + t) * 128, 128), 128), :]
+            ins[at, :] = jnp.dot(these, weights, preferred_element_type=F32)
 
     def store(c):
         at = pl.ds(pl.multiple_of(c * part, part), part)
@@ -707,19 +737,17 @@
             pl.when(edge)(lambda: next_edges(s))
         else:
 
-            def put(g):
-                flat = strip[pl.ds(pl.multiple_of(g * 128, 128), 128), :].T.astype(BF16)
-                for t in range(16):
-                    at = pl.ds(pl.multiple_of(g * 2048 + t * 128, 128), 128)
-                    ins[at, :] = jnp.dot(flat, back[t], preferred_element_type=F32)
-
-            loop(0, groups, put)
+            for g in range(groups):
+                flat[g * 128 : g * 128 + 128, :] = strip[g * 128 : g * 128 + 128, :].T.astype(BF16)
+            bring_back(0)
 
         def chunk(c):
             fill_main(s, c)
 
             def one(ky):
                 main_row(ky, s, b_of)
+                if s == SWEEPS - 1:
+                    bring_back(jnp.minimum(ky + 1, kyn - 1))
                 if s < SWEEPS - 1:
                     pack_halo(ky, s + 1)
 
@@ -787,6 +815,7 @@
         vm((hr, 128), F32), vm((xr, 128), F32), vm((xr, 128), F32),
         vm((ur, 128), F32), vm((ur, 128), F32), vm((ur, 128), F32),
         vm((32, 128), F32), vm((24, 128), F32), vm((rows * 8, 128), F32),
+        vm((kyn * 32, 128), BF16), vm((2048, 128), BF16),
         vm((8, 128), F32), vm((2, 128), jnp.int32), vm((2, 8), jnp.int32),
         vm((rows * 2, 128), BF16), vm((2, 8, rows), BF16),
         dma((CHUNKS,)), dma((5,)), dma((CHUNKS,)), dma((nv - 1,)), dma((nv - 1,)),

time: 32.6 us -> 31 us (0.951)
  Pallas kernels: 29.4 us -> 27.8 us
    pallas_call x1, Pallas kernels: 29.4 us -> 27.8 us  [body(): pl.pallas_call(functools.partial(kernel, nv, nx, ny, rows), out_shape=jax...]
where the time goes in v2:
time: 31 us; the launch traced here: 30.8 us
  Pallas kernels  27.8 us (90%)
  local copies, waits for them, and re-layouts  3.05 us (10%)
    pallas_call x1, Pallas kernels, body(): pl.pallas_call(functools.partial(kernel, nv, nx, ny, rows), out_shape=jax...  27.8 us
    unnamed x1, local copies, waits for them, and re-layouts  3.05 us

profile of v2, /device:TPU:96, one launch (start us, length us, event | category | flops | bytes accessed | tf_op | source)
XLA Modules:
  0.0 30.8 jit_solution(16891050627494310987)
XLA Ops:
  0.0 27.8 %bgk_step.1 = bf16[8192,128]{1,0:T(8,128)(2,1)} custom-call(bf16[8192,128]{1,0:T(8,128)(2,1)} %bitcast.5, f32[8,128]{1,0:T(8,128)} %relax_h.1, s32[2,128]{1,0:T(2,128)} %lrk_h.1, s32[2,8]{1,0:T(2,128)} %btk_h.1, bf16[2048,128]{1,0:T(8,128)(2,1)} %bitcast.6, bf16[2,8,1024]{2,1,0:T(8,128)(2,1)} %bitcast.7), custom_call_target="tpu_custom_call" | custom-call | tf_op jit(solution)/shard_map/bgk_step/pallas_call | solution.py:828
  27.8 3.0 %copy.8 = bf16[1024,8,128]{2,1,0:T(8,128)(2,1)} copy(bf16[1024,8,128]{2,1,0:T(8,128)(2,1)} %bitcast.4) | data formatting | bytes 4194304

commit v3 on v2

--- a/solution.py
+++ b/solution.py
@@ -14,6 +14,7 @@
 NEWTON = 2
 SWEEPS = 4
 CHUNKS = 4
+PARTS = 8
 STEP = 12.0 / NVX
 WEIGHT = STEP * STEP / (2.0 * math.pi)
 DT_INV = (NVX - 1) * STEP / 100.0
@@ -786,6 +787,26 @@
     loop(0, SWEEPS, drain)
     for c in range(CHUNKS):
         store(c).wait()
+
+
+def hand_over(src_h, dst_h, held, come, go):
+    part = src_h.shape[0] // PARTS
+
+    def copy_in(n):
+        at = pl.ds(n * part, part)
+        return pltpu.make_async_copy(src_h.at[at], held.at[at], come.at[n])
+
+    def copy_out(n):
+        at = pl.ds(n * part, part)
+        return pltpu.make_async_copy(held.at[at], dst_h.at[at], go.at[n])
+
+    for n in range(PARTS):
+        copy_in(n).start()
+    for n in range(PARTS):
+        copy_in(n).wait()
+        copy_out(n).start()
+    for n in range(PARTS):
+        copy_out(n).wait()
 
 
 def body(previous, relax_time, left_right_kind, bottom_top_kind, left_right_inflow, bottom_top_inflow, *, sizes):
@@ -843,6 +864,15 @@
         left_right_inflow.reshape(rows * 2, 128),
         bottom_top_inflow.transpose(1, 2, 0),
     )
+    out = pl.pallas_call(
+        hand_over,
+        out_shape=jax.ShapeDtypeStruct((rows * 8, 128), BF16),
+        in_specs=[far],
+        out_specs=far,
+        scratch_shapes=[pltpu.VMEM((rows * 8, 128), BF16), pltpu.SemaphoreType.DMA((PARTS,)), pltpu.SemaphoreType.DMA((PARTS,))],
+        compiler_params=pltpu.CompilerParams(vmem_limit_bytes=62 * 1024 * 1024),
+        name="hand_over",
+    )(out)
     return out.reshape(rows, cx, cy)
 
 

time: 31 us -> 30.3 us (0.977)
  local copies, waits for them, and re-layouts: 3.05 us -> 0 us
  Pallas kernels: 27.8 us -> 30.2 us
    unnamed x1 -> x0, local copies, waits for them, and re-layouts: 3.05 us -> none
    pallas_call x0 -> x1, Pallas kernels: none -> 2.39 us  [body(): pl.pallas_call(hand_over, out_shape=jax.ShapeDtypeStruct((rows * 8, 128),...]
where the time goes in v3:
time: 30.3 us; the launch traced here: 30.2 us
  Pallas kernels  30.2 us (100%)
    pallas_call x1, Pallas kernels, body(): pl.pallas_call(functools.partial(kernel, nv, nx, ny, rows), out_shape=jax...  27.8 us
    pallas_call x1, Pallas kernels, body(): pl.pallas_call(hand_over, out_shape=jax.ShapeDtypeStruct((rows * 8, 128),...  2.39 us

profile of v3, /device:TPU:96, one launch (start us, length us, event | category | flops | bytes accessed | tf_op | source)
XLA Modules:
  0.0 30.2 jit_solution(931119412326116346)
XLA Ops:
  0.0 27.8 %bgk_step.1.src_h = bf16[8192,128]{1,0:T(8,128)(2,1)} custom-call(bf16[8192,128]{1,0:T(8,128)(2,1)} %bitcast.4, f32[8,128]{1,0:T(8,128)} %relax_h.1, s32[2,128]{1,0:T(2,128)} %lrk_h.1, s32[2,8]{1,0:T(2,128)} %btk_h.1, bf16[2048,128]{1,0:T(8,128)(2,1)} %bitcast.5, bf16[2,8,1024]{2,1,0:T(8,128)(2,1)} %bitcast.6), custom_call_target="tpu_custom_call" | custom-call | tf_op jit(solution)/shard_map/bgk_step/pallas_call | solution.py:849
  27.8 2.4 %hand_over.1 = bf16[8192,128]{1,0:T(8,128)(2,1)} custom-call(bf16[8192,128]{1,0:T(8,128)(2,1)} %bgk_step.1.src_h), custom_call_target="tpu_custom_call" | custom-call | tf_op jit(solution)/shard_map/hand_over/pallas_call | solution.py:867

commit v4 on v3

--- a/solution.py
+++ b/solution.py
@@ -13,7 +13,7 @@
 HALF = NVX // 2
 NEWTON = 2
 SWEEPS = 4
-CHUNKS = 4
+CHUNKS = 8
 PARTS = 8
 STEP = 12.0 / NVX
 WEIGHT = STEP * STEP / (2.0 * math.pi)
@@ -270,7 +270,9 @@
 
     def take_chunk(c, u):
         load(c).wait()
-        return lax.fori_loop(c * per, c * per + per, take_row, u)
+        for r in range(per):
+            u = take_row(c * per + r, u)
+        return u
 
     zero = jnp.zeros((8, 128), F32)
     u = lax.fori_loop(0, CHUNKS, take_chunk, (zero, zero, zero, zero))
@@ -528,8 +530,8 @@
             for k in range(1, half):
                 total = total + fyr[s, k]
             flux = jnp.broadcast_to(jnp.sum(total, axis=0, keepdims=True), (8, 128))
-            for k in (8, 16, 32, 64):
-                flux = flux + pltpu.roll(flux, k, 1)
+            for k in (8, 32):
+                flux = (flux + pltpu.roll(flux, k, 1)) + (pltpu.roll(flux, 2 * k, 1) + pltpu.roll(flux, 3 * k, 1))
             flux = flux * kinds[16:24, :]
             for b in range(kyn * 4 // 8):
                 at = slice(b * 8, b * 8 + 8)
@@ -571,7 +573,8 @@
             if s < SWEEPS - 1:
                 pack_strips(s + 1, g, tiles)
 
-        loop(0, groups // 2, step)
+        for g in range(groups // 2):
+            step(g)
 
     def next_edges(s):
         off = jnp.where(first, 0, PITCH * HALF + 8)
@@ -752,7 +755,8 @@
                 if s < SWEEPS - 1:
                     pack_halo(ky, s + 1)
 
-            loop(c * per, c * per + per, one)
+            for r in range(per):
+                one(c * per + r)
             if s < SWEEPS - 1:
                 send_chunk(s + 1, c)
             else:

time: 30.3 us -> 28.8 us (0.950)
  Pallas kernels: 30.2 us -> 28.7 us
    pallas_call x1, Pallas kernels: 27.8 us -> 26.3 us  [body(): pl.pallas_call(functools.partial(kernel, nv, nx, ny, rows), out_shape=jax...]
where the time goes in v4:
time: 28.8 us; the launch traced here: 28.7 us
  Pallas kernels  28.7 us (100%)
    pallas_call x1, Pallas kernels, body(): pl.pallas_call(functools.partial(kernel, nv, nx, ny, rows), out_shape=jax...  26.3 us
    pallas_call x1, Pallas kernels, body(): pl.pallas_call(hand_over, out_shape=jax.ShapeDtypeStruct((rows * 8, 128),...  2.39 us

profile of v4, /device:TPU:96, one launch (start us, length us, event | category | flops | bytes accessed | tf_op | source)
XLA Modules:
  0.0 28.7 jit_solution(13332471460231232791)
XLA Ops:
  0.0 26.3 %bgk_step.1.src_h = bf16[8192,128]{1,0:T(8,128)(2,1)} custom-call(bf16[8192,128]{1,0:T(8,128)(2,1)} %bitcast.4, f32[8,128]{1,0:T(8,128)} %relax_h.1, s32[2,128]{1,0:T(2,128)} %lrk_h.1, s32[2,8]{1,0:T(2,128)} %btk_h.1, bf16[2048,128]{1,0:T(8,128)(2,1)} %bitcast.5, bf16[2,8,1024]{2,1,0:T(8,128)(2,1)} %bitcast.6), custom_call_target="tpu_custom_call" | custom-call | tf_op jit(solution)/shard_map/bgk_step/pallas_call | solution.py:853
  26.3 2.4 %hand_over.1 = bf16[8192,128]{1,0:T(8,128)(2,1)} custom-call(bf16[8192,128]{1,0:T(8,128)(2,1)} %bgk_step.1.src_h), custom_call_target="tpu_custom_call" | custom-call | tf_op jit(solution)/shard_map/hand_over/pallas_call | solution.py:871

commit v5 on v4

--- a/solution.py
+++ b/solution.py
@@ -620,7 +620,9 @@
                     thin_sum[h] = thin_sum[h] + strip[tile(ky, kx0 // 16 + h), :]
             return (*main, *thin_sum)
 
-        got = lax.fori_loop(0, groups, add, (zero,) * 6)
+        got = (zero,) * 6
+        for g in range(groups):
+            got = add(g, got)
         main = thin = zero
         for q in range(HALF // 8):
             main = main + got[q] * speeds[q]
@@ -824,12 +826,12 @@
     ur = kyn * 4
     xr = kyn * 2
     scratch = [
-        vm((rows * 8, 128), BF16), vm((rows * PITCH, 128), F32), vm((rows * 8, 128), F32),
-        vm((NVX * 8, 128), F32), vm((NVX * 8, 128), F32),
+        vm((rows * 8, 128), BF16), vm((rows * PITCH + 72, 128), F32), vm((rows * 8, 128), F32),
+        vm((NVX * 8 + 64, 128), F32), vm((NVX * 8, 128), F32),
         vm((SWEEPS, hr, 128), BF16), vm((SWEEPS, hr, 128), BF16),
         vm((SWEEPS, hr, 128), BF16), vm((SWEEPS, hr, 128), BF16),
         vm((32, 128), F32), vm((nv - 1, 32, 128), F32),
-        vm((thin, 128), F32), vm((thin, 128), F32), vm((thin, 128), F32),
+        vm((thin + 64, 128), F32), vm((thin, 128), F32), vm((thin, 128), F32),
         vm((ur, 128), F32),
         vm((SWEEPS, xr, 128), BF16), vm((SWEEPS, xr, 128), BF16),
         vm((SWEEPS, xr, 128), BF16), vm((SWEEPS, xr, 128), BF16),

time: 28.8 us -> 28.9 us (level)
  no operation moved by 1% of the time
where the time goes in v5:
time: 28.9 us; the launch traced here: 28.7 us
  Pallas kernels  28.7 us (99%)
    pallas_call x1, Pallas kernels, body(): pl.pallas_call(functools.partial(kernel, nv, nx, ny, rows), out_shape=jax...  26.3 us
    pallas_call x1, Pallas kernels, body(): pl.pallas_call(hand_over, out_shape=jax.ShapeDtypeStruct((rows * 8, 128),...  2.39 us

profile of v5, /device:TPU:96, one launch (start us, length us, event | category | flops | bytes accessed | tf_op | source)
XLA Modules:
  0.0 28.7 jit_solution(6744520936415360895)
XLA Ops:
  0.0 26.3 %bgk_step.1.src_h = bf16[8192,128]{1,0:T(8,128)(2,1)} custom-call(bf16[8192,128]{1,0:T(8,128)(2,1)} %bitcast.4, f32[8,128]{1,0:T(8,128)} %relax_h.1, s32[2,128]{1,0:T(2,128)} %lrk_h.1, s32[2,8]{1,0:T(2,128)} %btk_h.1, bf16[2048,128]{1,0:T(8,128)(2,1)} %bitcast.5, bf16[2,8,1024]{2,1,0:T(8,128)(2,1)} %bitcast.6), custom_call_target="tpu_custom_call" | custom-call | tf_op jit(solution)/shard_map/bgk_step/pallas_call | solution.py:855
  26.3 2.4 %hand_over.1 = bf16[8192,128]{1,0:T(8,128)(2,1)} custom-call(bf16[8192,128]{1,0:T(8,128)(2,1)} %bgk_step.1.src_h), custom_call_target="tpu_custom_call" | custom-call | tf_op jit(solution)/shard_map/hand_over/pallas_call | solution.py:873
